TPU v7x, 32 devices: a whole 2x2x4 slice. The times are simulated.
32 devices in a mesh: groups: 2 (over x), expert: 16 (over z, y, core).
Axes of the slice: x: 2, y: 2, z: 4, core: 2. Of those that a mesh axis runs over, the one named last changes fastest.
Arguments:
- hidden: bfloat16 [2048, 4096], P(('groups', 'expert')), parts along dimension 0, may hold values from -6 to 6
- norm_gain: bfloat16 [4096], replicated, may hold values from 0.099609375 to 1.8984375
- routes: int32 [2048, 8], P(('groups', 'expert')), parts along dimension 0, may hold values from 0 to 7, as said below
- gate_vals: float32 [2048, 8], P(('groups', 'expert')), parts along dimension 0, may hold values from 0.02 to 0.3
- span_len: int32 [32], P('groups'), parts along dimension 0, may hold values from 33 to 64, as said below
- w_gate: bfloat16 [16, 4096, 768], P('expert'), may hold values from -0.09375 to 0.09375
- w_up: bfloat16 [16, 4096, 768], P('expert'), may hold values from -0.09375 to 0.09375
- w_down: bfloat16 [16, 768, 4096], P('expert'), may hold values from -0.15625 to 0.15625
Outputs:
- output: bfloat16 [2048, 4096], P(('groups', 'expert')), parts along dimension 0
There are 2 independent parts, one for each index of `groups`. A program takes and returns all parts, laid end to end along the dimension named above; an argument that names none is the same for every part. Nothing has to cross between parts.
Inputs may be any that keep to these rules, and one draw needn't show every extreme that they name: `routes`: each row names 8 different experts. In the rows of one device no expert is named more than 64 times, live or not, and in every draw the live choices of some device name some expert exactly 64 times. `span_len`: in every draw some sequence has all 64 positions live.
All inputs are finite; a program needn't handle non-finite values.
Results may differ from a plain program's by a relative error of at most 0.0039.
Values may be sent and summed in bfloat16 or wider, within the bound.
A program may use at most 128 MiB of HBM per device.

v0:
```python
import jax
import jax.numpy as jnp
from jax import lax
from jax.sharding import PartitionSpec as P

SEQ_TOK = 64


def deliver(buffer):
    return lax.all_to_all(buffer, "expert", split_axis=0, concat_axis=0, tiled=True)


def expert_rows(rows, w_gate, w_up, w_down):
    gated = jnp.dot(rows, w_gate[0], preferred_element_type=jnp.float32)
    upper = jnp.dot(rows, w_up[0], preferred_element_type=jnp.float32)
    act = (jax.nn.silu(gated) * upper).astype(jnp.bfloat16)
    return jnp.dot(act, w_down[0], preferred_element_type=jnp.float32).astype(jnp.bfloat16)


def on_device(hidden, norm_gain, routes, gate_vals, span_len, w_gate, w_up, w_down):
    tok_rows, width = hidden.shape
    top_count = routes.shape[1]
    count_dev = lax.axis_size("expert")
    experts = count_dev // 2
    capacity = min(tok_rows, 2 * ((3 * tok_rows * top_count // (2 * experts) + 1) // 2))
    my_index = lax.axis_index("expert")
    values = hidden.astype(jnp.float32)
    scale = lax.rsqrt(jnp.mean(values * values, axis=-1, keepdims=True) + 1e-06)
    normed = (values * scale * norm_gain.astype(jnp.float32)).astype(jnp.bfloat16)
    position = my_index * tok_rows + jnp.arange(tok_rows, dtype=jnp.int32)
    seq_match = (position // SEQ_TOK)[:, None] == jnp.arange(span_len.shape[0], dtype=jnp.int32)[
        None, :
    ]
    seq_len = jnp.sum(jnp.where(seq_match, span_len[None, :], 0), axis=-1)
    live = position % SEQ_TOK < seq_len
    onehot = (
        (routes[:, :, None] == jnp.arange(experts, dtype=jnp.int32)[None, None, :])
        & live[:, None, None]
    ).astype(jnp.int32)
    flat = onehot.reshape(tok_rows * top_count, experts)
    rank = jnp.cumsum(flat, axis=0) - flat
    slot = jnp.sum(rank * flat, axis=-1).reshape(tok_rows, top_count)
    target = routes * capacity + slot
    place = (
        target[:, :, None] == jnp.arange(experts * capacity, dtype=jnp.int32)[None, None, :]
    ) & live[:, None, None]
    dispatch = jnp.any(place, axis=1).astype(jnp.bfloat16)
    outgoing = jnp.dot(dispatch.T, normed, preferred_element_type=jnp.float32).astype(jnp.bfloat16)
    copies = jnp.broadcast_to(
        outgoing.reshape(experts, 1, capacity, width), (experts, 2, capacity, width)
    ).reshape(count_dev, capacity, width)
    arrived = deliver(copies).reshape(count_dev * capacity, width)
    partial_value = expert_rows(arrived, w_gate, w_up, w_down).reshape(count_dev, capacity, width)
    returned = deliver(partial_value).reshape(experts, 2, capacity, width)
    results = (
        (returned[:, 0].astype(jnp.float32) + returned[:, 1].astype(jnp.float32))
        .astype(jnp.bfloat16)
        .reshape(experts * capacity, width)
    )
    weights = jnp.sum(jnp.where(place, gate_vals[:, :, None], 0.0), axis=1)
    moe = jnp.dot(weights, results.astype(jnp.float32), precision=lax.Precision.HIGHEST)
    return (values + moe).astype(jnp.bfloat16)


def solution(mesh):
    return jax.shard_map(
        on_device,
        mesh=mesh,
        in_specs=(
            P(("groups", "expert"), None),
            P(),
            P(("groups", "expert"), None),
            P(("groups", "expert"), None),
            P("groups"),
            P("expert", None, None),
            P("expert", None, None),
            P("expert", None, None),
        ),
        out_specs=P(("groups", "expert"), None),
        check_vma=False,
    )
```

profile of v0, /device:TPU:13, one launch (start us, length us, event | category | flops | bytes accessed | tf_op | source)
XLA Modules:
  0.0 423.4 jit_solution(17132665065129234321)
XLA Ops:
  0.0 0.7 select_reduce_fusion.1
  0.8 0.1 reduce_sum.39
  0.9 0.8 copy.21
  1.6 0.1 eq.61
  1.7 0.1 eq.54
  1.8 0.1 and.68
  1.9 0.1 and.69
  2.0 1.1 reduce-window.6
  3.2 0.2 slice_reduce_fusion
  3.4 0.1 and.63
  3.5 0.1 and.64
  3.6 0.1 fusion.17
  3.7 0.1 reshape.102
  3.8 0.1 copy.23
  3.9 0.7 multiply_add_fusion
  4.6 0.1 copy.24
  4.7 0.4 fusion.12
  5.1 0.7 convert_element_type.51
  5.8 1.2 fusion.8
  7.1 2.4 convolution_convert_fusion.1
  9.4 4.3 %broadcast_in_dim.48 = bf16[8,2,64,4096]{3,2,1,0:T(8,128)(2,1)} broadcast(bf16[8,64,4096]{2,1,0:T(8,128)(2,1)S(1)} %bitcast.32), dimensions={0,2,3} | broadcast | bytes 12582912 | tf_op jit(solution)/shard_map/broadcast_in_dim | solution.py:49
  13.7 188.9 %all_to_all.10 = bf16[16,64,4096]{2,1,0:T(8,128)(2,1)S(1)} all-to-all(bf16[16,64,4096]{2,1,0:T(8,128)(2,1)} %bitcast.31), channel_id=1, replica_groups=mesh['groups'=2,'expert'=16] {'expert'}, dimensions={0} | all-to-all | bytes 16777216 | tf_op jit(solution)/shard_map/all_to_all | solution.py:10
  202.7 9.2 %fusion.1 = f32[1024,768]{1,0:T(8,128)S(1)} fusion(bf16[1024,4096]{1,0:T(8,128)(2,1)S(1)} %bitcast.35, bf16[1,4096,768]{2,1,0:T(8,128)(2,1)} %param.14), kind=kOutput, calls=%fused_computation.3 | convolution fusion | flops 6442450944 | bytes 17825792 | tf_op jit(solution)/shard_map/dot_general | solution.py:15
  211.9 0.0 slice-start.3
  211.9 7.0 %multiply_convert_fusion = bf16[1024,768]{1,0:T(8,128)(2,1)S(1)} fusion(f32[1024,768]{1,0:T(8,128)S(1)} %fusion.1, bf16[1024,4096]{1,0:T(8,128)(2,1)S(1)} %bitcast.36, bf16[1,4096,768]{2,1,0:T(8,128)(2,1)S(1)} %bitcast.38), kind=kOutput, calls=%fused_computation.10 | convolution fusion | flops 6447169536 | bytes 19398656 | tf_op jit(solution)/shard_map/dot_general | solution.py:14
  218.9 8.8 %convolution_convert_fusion = bf16[1024,4096]{1,0:T(8,128)(2,1)} fusion(bf16[1024,768]{1,0:T(8,128)(2,1)S(1)} %multiply_convert_fusion, bf16[1,768,4096]{2,1,0:T(8,128)(2,1)S(1)} %bitcast.40), kind=kOutput, calls=%fused_computation.1 | convolution fusion | flops 6446645248 | bytes 16252928 | tf_op jit(solution)/shard_map/dot_general | solution.py:17
  227.7 5.8 %all-to-all-start.1 = ((bf16[16,64,4096]{2,1,0:T(8,128)(2,1)}), bf16[16,64,4096]{2,1,0:T(8,128)(2,1)}, u32[]{:S(2)}, u32[]{:S(2)}) async-start(bf16[16,64,4096]{2,1,0:T(8,128)(2,1)} %bitcast.34), calls=%async_computation.1 | async-start | bytes 16777216 | tf_op jit(solution)/shard_map/all_to_all | solution.py:10
  233.6 0.1 copy.25
  233.6 0.5 select_reduce_fusion
  234.1 181.8 %all-to-all-done.1 = bf16[16,64,4096]{2,1,0:T(8,128)(2,1)} async-done(((bf16[16,64,4096]{2,1,0:T(8,128)(2,1)}), bf16[16,64,4096]{2,1,0:T(8,128)(2,1)}, u32[]{:S(2)}, u32[]{:S(2)}) %all-to-all-start.1) | async-done | bytes 8388640 | tf_op jit(solution)/shard_map/all_to_all | solution.py:10
  415.9 4.3 %add_convert_fusion = bf16[8,1,64,4096]{3,2,1,0:T(8,128)(2,1)S(1)} fusion(bf16[8,2,64,4096]{3,2,1,0:T(8,128)(2,1)} %bitcast.9), kind=kLoop, calls=%fused_computation | loop fusion | flops 8388608 | bytes 12582912 | tf_op jit(solution)/shard_map/convert_element_type | solution.py:57
  420.3 3.1 fusion.5
  (20 shorter events, 0.1 us)
Async XLA Ops:
  13.7 198.1 %slice-start = ((s8[6291456]{0:T(1024)(128)(4,1)}), s8[4194304]{0:T(1024)(128)(4,1)S(1)}, s32[]{:S(2)}) async-start(s8[6291456]{0:T(1024)(128)(4,1)} %bitcast.37), calls=%async_computation.2 | async-start | bytes 8388608
  202.7 9.2 %slice-start.1 = ((s8[6291456]{0:T(1024)(128)(4,1)}), s8[2097152]{0:T(1024)(128)(4,1)S(1)}, s32[]{:S(2)}) async-start(s8[6291456]{0:T(1024)(128)(4,1)} %bitcast.37), calls=%async_computation.3 | async-start | bytes 4194304
  202.7 16.2 %slice-start.2 = ((s8[6291456]{0:T(1024)(128)(4,1)}), s8[4194304]{0:T(1024)(128)(4,1)S(1)}, s32[]{:S(2)}) async-start(s8[6291456]{0:T(1024)(128)(4,1)} %bitcast.39), calls=%async_computation.4 | async-start | bytes 8388608
  211.9 7.0 %slice-start.3 = ((s8[6291456]{0:T(1024)(128)(4,1)}), s8[2097152]{0:T(1024)(128)(4,1)S(1)}, s32[]{:S(2)}) async-start(s8[6291456]{0:T(1024)(128)(4,1)} %bitcast.39), calls=%async_computation.5 | async-start | bytes 4194304
  227.7 5.8 %copy-start.1 = (f32[64,8]{0,1:T(8,128)S(1)}, f32[64,8]{0,1:T(8,128)}, u32[]{:S(2)}) copy-start(f32[64,8]{0,1:T(8,128)} %param.11) | copy-start | bytes 6148
  227.7 188.2 %all-to-all-start.1 = ((bf16[16,64,4096]{2,1,0:T(8,128)(2,1)}), bf16[16,64,4096]{2,1,0:T(8,128)(2,1)}, u32[]{:S(2)}, u32[]{:S(2)}) async-start(bf16[16,64,4096]{2,1,0:T(8,128)(2,1)} %bitcast.34), calls=%async_computation.1 | async-start | bytes 16777216 | tf_op jit(solution)/shard_map/all_to_all | solution.py:10
  415.9 4.3 %copy-start = (bf16[64,4096]{1,0:T(8,128)(2,1)S(1)}, bf16[64,4096]{1,0:T(8,128)(2,1)}, u32[]{:S(2)}) copy-start(bf16[64,4096]{1,0:T(8,128)(2,1)} %param.8) | copy-start | bytes 1572868
where the time goes:
time: 424 us; the launch traced here: 423 us
  blocking collectives  189 us (45%)
  waiting for transfers between devices  182 us (43%)
  matrix products  30.4 us (7%)
  other arithmetic  9.96 us (2%)
  local copies, waits for them, and re-layouts  6.25 us (1%)
  starting transfers between devices  5.84 us (1%)
    all_to_all x1, blocking collectives, deliver(): lax.all_to_all(buffer, 'expert', split_axis=0, concat_axis=0, tiled=True)  189 us
    all_to_all x1, waiting for transfers between devices, deliver(): lax.all_to_all(buffer, 'expert', split_axis=0, concat_axis=0, tiled=True)  182 us
    dot_general x1, matrix products, expert_rows(): upper = jnp.dot(rows, w_up[0], preferred_element_type=jnp.float32)  9.15 us
    dot_general x1, matrix products, expert_rows(): jnp.dot(act, w_down[0], preferred_element_type=jnp.float32)  8.82 us
  transfers between devices with their start and end apart: 1, of which 1 were waited for; matrix products, arithmetic and copies ran while one was open for 0% of the time, Pallas kernels for 0%

commit v1 on v0

v1 whole, which is shorter than its diff:
```python
import jax
import jax.numpy as jnp
from jax import lax
from jax.sharding import PartitionSpec as P

SEQ_TOK = 64


def on_device(hidden, norm_gain, routes, gate_vals, span_len, w_gate, w_up, w_down):
    tok_rows, width = hidden.shape
    count_dev = lax.axis_size("expert")
    experts = count_dev // 2
    my_index = lax.axis_index("expert")
    values = hidden.astype(jnp.float32)
    scale = lax.rsqrt(jnp.mean(values * values, axis=-1, keepdims=True) + 1e-06)
    normed = (values * scale * norm_gain.astype(jnp.float32)).astype(jnp.bfloat16)
    position = my_index * tok_rows + jnp.arange(tok_rows, dtype=jnp.int32)
    seq_match = (position // SEQ_TOK)[:, None] == jnp.arange(span_len.shape[0], dtype=jnp.int32)[
        None, :
    ]
    seq_len = jnp.sum(jnp.where(seq_match, span_len[None, :], 0), axis=-1)
    live = position % SEQ_TOK < seq_len
    chosen = (routes[:, :, None] == jnp.arange(experts, dtype=jnp.int32)[None, None, :]) & live[
        :, None, None
    ]
    weights = jnp.sum(jnp.where(chosen, gate_vals[:, :, None], 0.0), axis=1)
    weights = lax.all_gather(weights, "expert", axis=0, tiled=True)
    mine = jnp.arange(experts, dtype=jnp.int32)[None, :] == my_index // 2
    weight = jnp.sum(jnp.where(mine, weights, 0.0), axis=1, keepdims=True)
    rows = lax.all_gather(normed, "expert", axis=0, tiled=True)
    gated = jnp.dot(rows, w_gate[0], preferred_element_type=jnp.float32)
    upper = jnp.dot(rows, w_up[0], preferred_element_type=jnp.float32)
    act = (jax.nn.silu(gated) * upper).astype(jnp.bfloat16)
    part = jnp.dot(act, w_down[0], preferred_element_type=jnp.float32)
    part = (part * weight).astype(jnp.bfloat16)
    moe = lax.psum_scatter(part, "expert", scatter_dimension=0, tiled=True)
    return (values + moe.astype(jnp.float32)).astype(jnp.bfloat16)


def solution(mesh):
    return jax.shard_map(
        on_device,
        mesh=mesh,
        in_specs=(
            P(("groups", "expert"), None),
            P(),
            P(("groups", "expert"), None),
            P(("groups", "expert"), None),
            P("groups"),
            P("expert", None, None),
            P("expert", None, None),
            P("expert", None, None),
        ),
        out_specs=P(("groups", "expert"), None),
        check_vma=False,
    )
```

time: 424 us -> 230 us (0.54)
  the two profiles are of different devices: /device:TPU:13 before, /device:TPU:0 now
where the time goes in v1:
time: 230 us
  waiting for transfers between devices  155 us (67%)
  matrix products  29.8 us (13%)
  blocking collectives  23.7 us (10%)
  between operations  13.5 us (6%)
  other arithmetic  7.53 us (3%)
    reduce_scatter x1, waiting for transfers between devices, on_device(): moe = lax.psum_scatter(part, 'expert', scatter_dimension=0, tiled=True)  103 us
    all_gather x1, waiting for transfers between devices, on_device(): rows = lax.all_gather(normed, 'expert', axis=0, tiled=True)  52.4 us
    all_gather x1, blocking collectives, on_device(): weights = lax.all_gather(weights, 'expert', axis=0, tiled=True)  23.7 us
    dot_general x1, matrix products, on_device(): upper = jnp.dot(rows, w_up[0], preferred_element_type=jnp.float32)  11 us
    dot_general x1, matrix products, on_device(): gated = jnp.dot(rows, w_gate[0], preferred_element_type=jnp.float32)  9.94 us
    dot_general x1, matrix products, on_device(): part = jnp.dot(act, w_down[0], preferred_element_type=jnp.float32)  8.87 us
  transfers between devices with their start and end apart: 2, of which 2 were waited for; matrix products, arithmetic and copies ran while one was open for 1% of the time, Pallas kernels for 0%

profile of v1, /device:TPU:0, one launch (start us, length us, event | category | flops | bytes accessed | tf_op | source)
XLA Modules:
  0.0 230.1 jit_solution(4950732853853442248)
XLA Ops:
  6.5 0.0 all-gather.3.cloned.1.call-start
  6.5 1.2 fusion.7
  7.8 0.7 convert_element_type.22
  8.5 2.0 fusion.9
  10.5 0.0 all-gather.3.cloned.1.call-update
  10.6 0.0 reduce-scatter.2.cloned.1.call-start
  10.6 0.7 select_reduce_fusion.2
  11.4 0.7 select_reduce_fusion.1
  12.1 23.7 %all-gather = f32[16,64,8]{1,2,0:T(8,128)S(1)} all-gather(f32[1,64,8]{1,2,0:T(8,128)S(1)} %bitcast.17), channel_id=1, replica_groups=mesh['groups'=2,'expert'=16] {'expert'}, dimensions={0}, use_global_device_ids=true | all-gather | bytes 34816 | tf_op jit(solution)/shard_map/all_gather | solution.py:27
  35.9 0.1 reshape.56
  36.0 0.1 select_reduce_fusion
  36.1 52.4 %all-gather.3.cloned.1.call-done = bf16[1024,4096]{1,0:T(8,128)(2,1)} async-done(((bf16[64,4096]{1,0:T(8,128)(2,1)}), bf16[1024,4096]{1,0:T(8,128)(2,1)}) %all-gather.3.cloned.1.call-update) | async-done | bytes 8388624 | tf_op jit(solution)/shard_map/all_gather | solution.py:30
  88.4 0.0 copy-start.1
  88.4 0.0 slice-start
  88.4 11.0 %fusion.1 = f32[1024,768]{1,0:T(8,128)S(1)} fusion(bf16[1024,4096]{1,0:T(8,128)(2,1)} %all-gather.3.cloned.1.call-done, bf16[1,4096,768]{2,1,0:T(8,128)(2,1)} %param.14), kind=kOutput, calls=%fused_computation.2 | convolution fusion | flops 6442450944 | bytes 17825792 | tf_op jit(solution)/shard_map/dot_general | solution.py:32
  99.5 0.0 copy-done.1
  99.5 0.0 slice-start.1
  99.5 9.9 %multiply_convert_fusion.1 = bf16[1024,768]{1,0:T(8,128)(2,1)S(1)} fusion(f32[1024,768]{1,0:T(8,128)S(1)} %fusion.1, bf16[1024,4096]{1,0:T(8,128)(2,1)S(1)} %copy-done.1, bf16[1,4096,768]{2,1,0:T(8,128)(2,1)} %param.13), kind=kOutput, calls=%fused_computation.6 | convolution fusion | flops 6447169536 | bytes 19398656 | tf_op jit(solution)/shard_map/dot_general | solution.py:31
  109.5 0.0 slice-done
  109.5 0.0 slice-done.1
  109.5 8.9 %multiply_convert_fusion = bf16[1024,4096]{1,0:T(8,128)(2,1)} fusion(f32[1024]{0:T(1024)S(1)} %select_reduce_fusion, bf16[1024,768]{1,0:T(8,128)(2,1)S(1)} %multiply_convert_fusion.1, bf16[1,768,4096]{2,1,0:T(8,128)(2,1)S(1)} %bitcast.19), kind=kOutput, calls=%fused_computation | convolution fusion | flops 6450839552 | bytes 16257024 | tf_op jit(solution)/shard_map/dot_general | solution.py:34
  118.3 0.0 copy-start
  118.4 0.0 reduce-scatter.2.cloned.1.call-update
  118.4 103.0 %reduce-scatter.2.cloned.1.call-done = bf16[64,4096]{1,0:T(8,128)(2,1)} async-done(((bf16[1024,4096]{1,0:T(8,128)(2,1)}), bf16[64,4096]{1,0:T(8,128)(2,1)}) %reduce-scatter.2.cloned.1.call-update) | async-done | bytes 524304 | tf_op jit(solution)/shard_map/reduce_scatter | solution.py:36
  221.3 0.0 copy-done
  221.3 2.0 fusion.10
  (6 shorter events, 0.1 us)
Async XLA Ops:
  6.5 81.9 %all-gather.3.cloned.1.call-start = ((), (), s32[]{:S(2)}) async-start(), calls=%async_computation.1 | async-start | bytes 8912896 | tf_op jit(solution)/shard_map/all_gather | solution.py:30
  10.6 210.8 %reduce-scatter.2.cloned.1.call-start = ((), (), s32[]{:S(2)}) async-start(), calls=%async_computation.2 | async-start | bytes 8912896 | tf_op jit(solution)/shard_map/reduce_scatter | solution.py:36
  88.4 11.0 %copy-start.1 = (bf16[1024,4096]{1,0:T(8,128)(2,1)S(1)}, bf16[1024,4096]{1,0:T(8,128)(2,1)}, u32[]{:S(2)}) copy-start(bf16[1024,4096]{1,0:T(8,128)(2,1)} %all-gather.3.cloned.1.call-done) | copy-start | bytes 25165828
  88.4 21.0 %slice-start = ((s8[6291456]{0:T(1024)(128)(4,1)}), s8[4194304]{0:T(1024)(128)(4,1)S(1)}, s32[]{:S(2)}) async-start(s8[6291456]{0:T(1024)(128)(4,1)} %bitcast.18), calls=%async_computation.3 | async-start | bytes 8388608
  99.5 10.0 %slice-start.1 = ((s8[6291456]{0:T(1024)(128)(4,1)}), s8[2097152]{0:T(1024)(128)(4,1)S(1)}, s32[]{:S(2)}) async-start(s8[6291456]{0:T(1024)(128)(4,1)} %bitcast.18), calls=%async_computation.4 | async-start | bytes 4194304
  118.3 103.0 %copy-start = (bf16[64,4096]{1,0:T(8,128)(2,1)S(1)}, bf16[64,4096]{1,0:T(8,128)(2,1)}, u32[]{:S(2)}) copy-start(bf16[64,4096]{1,0:T(8,128)(2,1)} %param.8) | copy-start | bytes 1572868
Sparse Core Ops, SparseCore 0:
  10.7 77.7 all-gather.2
  118.5 102.8 reduce-scatter.1

commit v2 on v1

v2 whole, which is shorter than its diff:
```python
import functools

import jax
import jax.numpy as jnp
from jax import lax
from jax.experimental import pallas as pl
from jax.experimental.pallas import tpu as pltpu
from jax.sharding import PartitionSpec as P

SEQ_TOK = 64
EXTRA = 128
VMEM_BUDGET = 60 * 2**20
MESH = pl.DeviceIdType.MESH


def gate_weights(routes, gate_vals, live, lanes):
    columns = lax.broadcasted_iota(jnp.int32, (routes.shape[0], lanes), 1)
    total = jnp.zeros((routes.shape[0], lanes), jnp.float32)
    for k in range(routes.shape[1]):
        total += jnp.where(columns == routes[:, k : k + 1], gate_vals[:, k : k + 1], 0.0)
    return jnp.where(live, total, 0.0)


def normalise(hidden, gain):
    values = hidden.astype(jnp.float32)
    scale = lax.rsqrt(jnp.mean(values * values, axis=-1, keepdims=True) + 1e-06)
    return (values * scale * gain.astype(jnp.float32)).astype(jnp.bfloat16)


def kernel(chips, snake, hidden, gain, routes, gate_vals, span_len, w_gate, w_up, w_down, out,
           x, part, peer_part, arrived, act, wg, wu, wd,
           w_sem, ag_send, ag_recv, agp_send, agp_recv, rs_send, rs_recv, rsp_send, rsp_recv):
    tok, width = hidden.shape
    ff = wg.shape[1]
    half = tok // 2
    far = chips // 2
    me = lax.axis_index("expert")
    chip, core = me // 2, me % 2

    def chip_at(place):
        if not snake:
            return place
        back = place // far
        return 2 * ((1 - back) * place + back * (chips - 1 - place)) + back

    if snake:
        row, deep = chip % 2, chip // 2
        place = (1 - row) * deep + row * (chips - 1 - deep)
    else:
        place = chip
    right = chip_at((place + 1) % chips) * 2 + core
    left = chip_at((place + chips - 1) % chips) * 2 + core
    peer = chip * 2 + 1 - core

    loads = [
        pltpu.make_async_copy(src.at[0], dst, w_sem.at[i])
        for i, (src, dst) in enumerate(((w_gate, wg), (w_up, wu), (w_down, wd)))
    ]
    for load in loads:
        load.start()

    barrier = pltpu.get_barrier_semaphore()
    for other in (left, right, peer):
        pl.semaphore_signal(barrier, inc=1, device_id={"expert": other}, device_id_type=MESH)

    x[0:tok, 0:width] = normalise(hidden[...], gain[...])
    first = me * tok
    offset = first % SEQ_TOK + lax.broadcasted_iota(jnp.int32, (tok, EXTRA // 2), 0)
    live = offset < span_len[first // SEQ_TOK]
    weights = gate_weights(routes[...], gate_vals[...], live, EXTRA // 2)
    upper = weights.astype(jnp.bfloat16)
    lower = (weights - upper.astype(jnp.float32)).astype(jnp.bfloat16)
    x[0:tok, width : width + EXTRA] = jnp.concatenate([upper, lower], axis=1)
    pl.semaphore_wait(barrier, 3)

    last = chips - 1

    def slot(s, d):
        return last if s == far - 1 else 1 + 2 * s + d

    onward = (right, left)
    homeward = (left, right)
    pending = []

    def rows(k, h):
        return pl.ds(2 * tok * k + half * h, half)

    def send_ring(k, s, d, h):
        copy = pltpu.make_async_remote_copy(
            src_ref=x.at[rows(k, h)], dst_ref=x.at[rows(slot(s, d), h)],
            send_sem=ag_send.at[d, s, h], recv_sem=ag_recv.at[d, s, h],
            device_id={"expert": onward[d]}, device_id_type=MESH)
        copy.start()
        pending.append(copy)

    def ring_copy(s, d, h):
        return pltpu.make_async_remote_copy(
            src_ref=x.at[rows(slot(s, d), h)], dst_ref=x.at[rows(slot(s, d), h)],
            send_sem=ag_send.at[d, s, h], recv_sem=ag_recv.at[d, s, h],
            device_id={"expert": onward[d]}, device_id_type=MESH)

    def peer_copy(k, h):
        return pltpu.make_async_remote_copy(
            src_ref=x.at[rows(k, h)], dst_ref=x.at[pl.ds(2 * tok * k + tok + half * h, half)],
            send_sem=agp_send.at[k, h], recv_sem=agp_recv.at[k, h],
            device_id={"expert": peer}, device_id_type=MESH)

    def send_peer(k, h):
        copy = peer_copy(k, h)
        copy.start()
        pending.append(copy)

    def part_copy(k):
        return pltpu.make_async_remote_copy(
            src_ref=part.at[pl.ds(2 * tok * k + tok, tok)], dst_ref=peer_part.at[pl.ds(tok * k, tok)],
            send_sem=rsp_send.at[k], recv_sem=rsp_recv.at[k],
            device_id={"expert": peer}, device_id_type=MESH)

    def compute(start, count):
        block = pl.ds(start, count)
        marks = x[block, width : width + EXTRA].astype(jnp.float32)
        lane = lax.broadcasted_iota(jnp.int32, marks.shape, 1) % (EXTRA // 2)
        weight = jnp.sum(jnp.where(lane == chip, marks, 0.0), axis=1, keepdims=True)
        tile = min(256, ff)

        @pl.loop(0, ff // tile)
        def _(j):
            cols = pl.ds(pl.multiple_of(j * tile, tile), tile)
            rows_in = x[block, 0:width]
            gated = jnp.dot(rows_in, wg[:, cols], preferred_element_type=jnp.float32)
            upped = jnp.dot(rows_in, wu[:, cols], preferred_element_type=jnp.float32)
            act[0:count, cols] = (gated / (1.0 + jnp.exp(-gated)) * upped).astype(jnp.bfloat16)

        wide = min(512, width)

        @pl.loop(0, width // wide)
        def _(j):
            cols = pl.ds(pl.multiple_of(j * wide, wide), wide)
            product = jnp.dot(act[0:count, :], wd[:, cols], preferred_element_type=jnp.float32)
            part[block, cols] = (product * weight).astype(jnp.bfloat16)

        for k in range(start // (2 * tok), (start + count) // (2 * tok)):
            copy = part_copy(k)
            copy.start()
            pending.append(copy)

    for h in range(2):
        for d in range(2):
            send_ring(0, 0, d, h)
        send_peer(0, h)
    for load in loads:
        load.wait()
    for h in range(2):
        peer_copy(0, h).wait_recv()
    compute(0, 2 * tok)

    for s in range(far):
        for h in range(2):
            for d in range(2):
                if s == far - 1 and h != d:
                    continue
                k = slot(s, d)
                ring_copy(s, d, h).wait_recv()
                if s + 1 < far - 1 or (s + 1 == far - 1 and h == d):
                    send_ring(k, s + 1, d, h)
                send_peer(k, h)
        for k in sorted({slot(s, 0), slot(s, 1)}):
            for h in range(2):
                peer_copy(k, h).wait_recv()
        if s < far - 1:
            compute(2 * tok * slot(s, 0), 4 * tok)
        else:
            compute(2 * tok * last, 2 * tok)

    def place_of(s, d, h):
        k = slot(s, d) if s >= 0 else (last if d else 0)
        return arrived.at[pl.ds(tok * k + half * h, half)]

    def sum_copy(s, d, h):
        return pltpu.make_async_remote_copy(
            src_ref=part.at[rows(slot(s, d), h)], dst_ref=place_of(s - 1, d, h),
            send_sem=rs_send.at[d, s, h], recv_sem=rs_recv.at[d, s, h],
            device_id={"expert": homeward[d]}, device_id_type=MESH)

    def local_sum(k, h):
        mine = part[rows(k, h), :].astype(jnp.float32)
        return mine + peer_part[pl.ds(tok * k + half * h, half), :].astype(jnp.float32)

    def send_sum(s, d, h):
        k = slot(s, d)
        total = local_sum(k, h)
        if s < far - 2 or (s == far - 2 and h == d):
            sum_copy(s + 1, d, h).wait_recv()
            total += place_of(s, d, h)[...].astype(jnp.float32)
        part[rows(k, h), :] = total.astype(jnp.bfloat16)
        copy = sum_copy(s, d, h)
        copy.start()
        pending.append(copy)

    for d in range(2):
        part_copy(slot(far - 2, d)).wait_recv()
        send_sum(far - 2, d, 1 - d)
    part_copy(last).wait_recv()
    for d in range(2):
        send_sum(far - 1, d, d)
    for d in range(2):
        send_sum(far - 2, d, d)
    for s in range(far - 3, -1, -1):
        for d in range(2):
            part_copy(slot(s, d)).wait_recv()
        for flip in (1, 0):
            for d in range(2):
                send_sum(s, d, d ^ flip)
    part_copy(0).wait_recv()
    for h in range(2):
        for d in range(2):
            sum_copy(0, d, h).wait_recv()
        total = local_sum(0, h)
        for d in range(2):
            total += place_of(-1, d, h)[...].astype(jnp.float32)
        here = slice(half * h, half * (h + 1))
        out[here, :] = (hidden[here, :].astype(jnp.float32) + total).astype(out.dtype)
    for copy in pending:
        copy.wait_send()


def vmem_need(tok, width, ff, chips):
    gathered = 2 * chips * tok
    return 2 * (gathered * (3 * width + EXTRA) + 3 * width * ff + 16 * tok * width)


def fused(snake, hidden, norm_gain, routes, gate_vals, span_len, w_gate, w_up, w_down):
    tok, width = hidden.shape
    ff = w_gate.shape[2]
    chips = lax.axis_size("expert") // 2
    far = chips // 2
    dma = pltpu.SemaphoreType.DMA
    in_vmem = pl.BlockSpec(memory_space=pltpu.VMEM)
    in_hbm = pl.BlockSpec(memory_space=pl.ANY)
    flops = 2 * 3 * 2 * chips * tok * width * ff
    return pl.pallas_call(
        functools.partial(kernel, chips, snake),
        out_shape=jax.ShapeDtypeStruct((tok, width), hidden.dtype),
        in_specs=[in_vmem] * 4 + [pl.BlockSpec(memory_space=pltpu.SMEM)] + [in_hbm] * 3,
        out_specs=in_vmem,
        scratch_shapes=[
            pltpu.VMEM((2 * chips * tok, width + EXTRA), jnp.bfloat16),
            pltpu.VMEM((2 * chips * tok, width), jnp.bfloat16),
            pltpu.VMEM((chips * tok, width), jnp.bfloat16),
            pltpu.VMEM((chips * tok, width), jnp.bfloat16),
            pltpu.VMEM((4 * tok, ff), jnp.bfloat16),
            pltpu.VMEM((width, ff), jnp.bfloat16),
            pltpu.VMEM((width, ff), jnp.bfloat16),
            pltpu.VMEM((ff, width), jnp.bfloat16),
            dma((3,)),
            dma((2, far, 2)), dma((2, far, 2)), dma((chips, 2)), dma((chips, 2)),
            dma((2, far, 2)), dma((2, far, 2)), dma((chips,)), dma((chips,)),
        ],
        compiler_params=pltpu.CompilerParams(
            collective_id=0, has_side_effects=True, vmem_limit_bytes=VMEM_BUDGET
        ),
        cost_estimate=pl.CostEstimate(
            flops=flops, bytes_accessed=6 * width * ff, transcendentals=2 * chips * tok * ff
        ),
    )(hidden, norm_gain.reshape(1, width), routes, gate_vals, span_len, w_gate, w_up, w_down)


def with_collectives(hidden, norm_gain, routes, gate_vals, span_len, w_gate, w_up, w_down):
    tok = hidden.shape[0]
    experts = lax.axis_size("expert") // 2
    me = lax.axis_index("expert")
    position = me * tok + jnp.arange(tok, dtype=jnp.int32)
    live = position % SEQ_TOK < span_len[position // SEQ_TOK]
    weights = gate_weights(routes, gate_vals, live[:, None], experts)
    weights = lax.all_gather(weights, "expert", axis=0, tiled=True)
    mine = jnp.arange(experts, dtype=jnp.int32)[None, :] == me // 2
    weight = jnp.sum(jnp.where(mine, weights, 0.0), axis=1, keepdims=True)
    rows = lax.all_gather(normalise(hidden, norm_gain), "expert", axis=0, tiled=True)
    gated = jnp.dot(rows, w_gate[0], preferred_element_type=jnp.float32)
    upper = jnp.dot(rows, w_up[0], preferred_element_type=jnp.float32)
    act = (jax.nn.silu(gated) * upper).astype(jnp.bfloat16)
    part = jnp.dot(act, w_down[0], preferred_element_type=jnp.float32)
    part = (part * weight).astype(jnp.bfloat16)
    moe = lax.psum_scatter(part, "expert", scatter_dimension=0, tiled=True)
    return (hidden.astype(jnp.float32) + moe.astype(jnp.float32)).astype(jnp.bfloat16)


def solution(mesh):
    devices = mesh.shape["expert"]

    def on_device(hidden, *rest):
        tok, width = hidden.shape
        fits = vmem_need(tok, width, rest[-1].shape[1], devices // 2) <= VMEM_BUDGET - 2**23
        if fits and devices % 4 == 0 and devices >= 12 and SEQ_TOK % tok == 0 and tok % 32 == 0:
            return fused(devices == 16, hidden, *rest)
        return with_collectives(hidden, *rest)

    return jax.shard_map(
        on_device,
        mesh=mesh,
        in_specs=(
            P(("groups", "expert"), None),
            P(),
            P(("groups", "expert"), None),
            P(("groups", "expert"), None),
            P("groups"),
            P("expert", None, None),
            P("expert", None, None),
            P("expert", None, None),
        ),
        out_specs=P(("groups", "expert"), None),
        check_vma=False,
    )
```

time: 230 us -> 109 us (0.47)
  waiting for transfers between devices: 155 us -> 0 us
  Pallas kernels: 0 us -> 103 us
  matrix products: 29.8 us -> 0 us
  blocking collectives: 23.7 us -> 0 us
  between operations: 13.5 us -> 0.01 us
  other arithmetic: 7.53 us -> 0 us
  local copies, waits for them, and re-layouts: 0.12 us -> 5.93 us
    reduce_scatter x1 -> x0, waiting for transfers between devices: 103 us -> none  [on_device(): moe = lax.psum_scatter(part, 'expert', scatter_dimension=0, tiled=True)]
    pallas_call x0 -> x1, Pallas kernels: none -> 103 us  [fused(): pl.pallas_call(functools.partial(kernel, chips, snake), out_shape=jax.Sha...]
    all_gather x1 -> x0, waiting for transfers between devices: 52.4 us -> none  [on_device(): rows = lax.all_gather(normed, 'expert', axis=0, tiled=True)]
    dot_general x3 -> x0, matrix products: 29.8 us -> none  [the longest x1 11 us: on_device(): upper = jnp.dot(rows, w_up[0], preferred_element_type=jnp.float32)]
    all_gather x1 -> x0, blocking collectives: 23.7 us -> none  [on_device(): weights = lax.all_gather(weights, 'expert', axis=0, tiled=True)]
    convert_element_type x3 -> x0, other arithmetic: 4.69 us -> none  [the longest x1 2.02 us: on_device(): (values * scale * norm_gain.astype(jnp.float32)).astype(jnp.bfloat16)]
    unnamed x9 -> x3, local copies, waits for them, and re-layouts: 0.1 us -> 4.62 us
    reduce_sum x4 -> x0, other arithmetic: 2.81 us -> none  [the longest x1 1.24 us: on_device(): scale = lax.rsqrt(jnp.mean(values * values, axis=-1, keepdims=True) + 1e-06)]
  transfers between devices with their start and end apart: 2 -> 0, of which waited for: 2 -> 0; matrix products, arithmetic and copies ran while one was open for 1% -> 0% of each run, Pallas kernels for 0% -> 0%
where the time goes in v2:
time: 109 us
  Pallas kernels  103 us (94%)
  local copies, waits for them, and re-layouts  5.93 us (5%)
    pallas_call x1, Pallas kernels, fused(): pl.pallas_call(functools.partial(kernel, chips, snake), out_shape=jax.Sha...  103 us
    unnamed x3, local copies, waits for them, and re-layouts  4.62 us

profile of v2, /device:TPU:0, one launch (start us, length us, event | category | flops | bytes accessed | tf_op | source)
XLA Modules:
  0.0 108.8 jit_solution(4800253269809440851)
XLA Ops:
  0.0 1.3 %reshape.3.gain = bf16[1,4096]{1,0:T(2,128)(2,1)} reshape(bf16[4096]{0:T(1024)(128)(2,1)} %param.9) | data formatting | bytes 16384 | tf_op jit(solution)/shard_map/reshape | solution.py:265
  1.3 1.4 %copy.9.routes = s32[64,8]{1,0:T(8,128)} copy(s32[64,8]{0,1:T(8,128)} %param.10) | data formatting | bytes 4096 | tf_op args[2]
  2.7 1.4 %copy.10.gate_vals = f32[64,8]{1,0:T(8,128)} copy(f32[64,8]{0,1:T(8,128)} %param.11) | data formatting | bytes 4096 | tf_op args[3]
  4.1 102.8 %shard_map.82 = bf16[64,4096]{1,0:T(8,128)(2,1)} custom-call(bf16[64,4096]{1,0:T(8,128)(2,1)} %hidden.1, bf16[1,4096]{1,0:T(2,128)(2,1)} %reshape.3.gain, s32[64,8]{1,0:T(8,128)} %copy.9.routes, f32[64,8]{1,0:T(8,128)} %copy.10.gate_vals, s32[16]{0:T(128)} %span_len.1, bf16[1,4096,768]{2,1,0:T(8,128)(2,1)} %w_gate.1, bf16[1,4096,768]{2,1,0:T(8,128)(2,1)} %w_up.1, ...), custom_call_target="tpu_custom_call" | custom-call | flops 19327352832 | bytes 18874368 | tf_op jit(solution)/shard_map/pallas_call | solution.py:241
  106.9 1.9 %copy.12 = bf16[64,4096]{1,0:T(8,128)(2,1)} copy(bf16[64,4096]{1,0:T(8,128)(2,1)} %shard_map.82) | data formatting | bytes 1048576

commit v3 on v2

v3 whole, which is shorter than its diff:
```python
import functools

import jax
import jax.numpy as jnp
from jax import lax
from jax.experimental import pallas as pl
from jax.experimental.pallas import tpu as pltpu
from jax.sharding import PartitionSpec as P

SEQ_TOK = 64
EXTRA = 128
VMEM_BUDGET = 60 * 2**20
MESH = pl.DeviceIdType.MESH


def gate_weights(routes, gate_vals, live, lanes):
    named = lax.broadcasted_iota(jnp.int32, (lanes, routes.shape[1]), 0)
    total = jnp.zeros((lanes, routes.shape[1]), jnp.float32)
    for k in range(routes.shape[0]):
        total += jnp.where(named == routes[k : k + 1, :], gate_vals[k : k + 1, :], 0.0)
    return jnp.where(live, total, 0.0)


def normalise(hidden, gain):
    values = hidden.astype(jnp.float32)
    scale = lax.rsqrt(jnp.mean(values * values, axis=-1, keepdims=True) + 1e-06)
    return (values * scale * gain.astype(jnp.float32)[None, :]).astype(jnp.bfloat16)


def kernel(chips, snake, hidden, gain, routes, gate_vals, span_len, w_gate, w_up, w_down, out,
           x, part, peer_part, arrived, act, wg, wu, wd,
           w_sem, ag_send, ag_recv, agp_send, agp_recv, rs_send, rs_recv, rsp_send, rsp_recv):
    tok, width = hidden.shape
    ff = wg.shape[1]
    half = tok // 2
    far = chips // 2
    me = lax.axis_index("expert")
    chip, core = me // 2, me % 2

    def chip_at(place):
        if not snake:
            return place
        back = place // far
        return 2 * ((1 - back) * place + back * (chips - 1 - place)) + back

    if snake:
        row, deep = chip % 2, chip // 2
        place = (1 - row) * deep + row * (chips - 1 - deep)
    else:
        place = chip
    right = chip_at((place + 1) % chips) * 2 + core
    left = chip_at((place + chips - 1) % chips) * 2 + core
    peer = chip * 2 + 1 - core

    loads = [
        pltpu.make_async_copy(src.at[0], dst, w_sem.at[i])
        for i, (src, dst) in enumerate(((w_gate, wg), (w_up, wu), (w_down, wd)))
    ]
    for load in loads:
        load.start()

    barrier = pltpu.get_barrier_semaphore()
    for other in (left, right, peer):
        pl.semaphore_signal(barrier, inc=1, device_id={"expert": other}, device_id_type=MESH)

    first = me * tok
    offset = first % SEQ_TOK + lax.broadcasted_iota(jnp.int32, (EXTRA // 2, tok), 1)
    live = offset < span_len[first // SEQ_TOK]
    weights = gate_weights(routes[...], gate_vals[...], live, EXTRA // 2)
    upper = weights.astype(jnp.bfloat16)
    lower = (weights - upper.astype(jnp.float32)).astype(jnp.bfloat16)
    same = lax.broadcasted_iota(jnp.int32, (tok, tok), 0) == lax.broadcasted_iota(
        jnp.int32, (tok, tok), 1
    )
    x[0:tok, width : width + EXTRA] = lax.dot_general(
        same.astype(jnp.bfloat16), jnp.concatenate([upper, lower], axis=0),
        (((1,), (1,)), ((), ())), preferred_element_type=jnp.float32,
    ).astype(jnp.bfloat16)

    last = chips - 1
    onward = (right, left)
    homeward = (left, right)
    pending = []

    def base(s, d, h, own):
        if s < 0:
            return (1 - own) * tok + h * half
        if s == far - 1:
            return 2 * tok * last + (1 - own) * tok + h * half
        return 2 * tok * (1 + 2 * s + (h ^ d)) + d * tok + (1 - own) * half

    def slot(s, d):
        return 0 if s < 0 else last if s == far - 1 else 1 + 2 * s + d

    def rows(s, d, h, own=1):
        return pl.ds(base(s, d, h, own), half)

    def begin(copy):
        copy.start()
        pending.append(copy)

    def ring_copy(s, d, h, source=None):
        return pltpu.make_async_remote_copy(
            src_ref=x.at[rows(s if source is None else source, d, h)], dst_ref=x.at[rows(s, d, h)],
            send_sem=ag_send.at[d, s, h], recv_sem=ag_recv.at[d, s, h],
            device_id={"expert": onward[d]}, device_id_type=MESH)

    def peer_copy(s, d, h):
        return pltpu.make_async_remote_copy(
            src_ref=x.at[rows(s, d, h)], dst_ref=x.at[rows(s, d, h, 0)],
            send_sem=agp_send.at[slot(s, d), h], recv_sem=agp_recv.at[slot(s, d), h],
            device_id={"expert": peer}, device_id_type=MESH)

    def held(s, d, h):
        return pl.ds(tok * slot(s, d) + half * h, half)

    def part_copy(s, d, h):
        return pltpu.make_async_remote_copy(
            src_ref=part.at[rows(s, d, h, 0)], dst_ref=peer_part.at[held(s, d, h)],
            send_sem=rsp_send.at[slot(s, d), h], recv_sem=rsp_recv.at[slot(s, d), h],
            device_id={"expert": peer}, device_id_type=MESH)

    def chunks(b):
        if b == 0:
            return [(-1, 0, 0), (-1, 0, 1)]
        if b == last:
            return [(far - 1, 0, 0), (far - 1, 1, 1)]
        s, f = (b - 1) // 2, (b - 1) % 2
        return [(s, 0, f), (s, 1, 1 - f)]

    def forward(b):
        for s, d, h in chunks(b):
            ring_copy(s, d, h).wait_recv()
            if s + 1 < far - 1 or (s + 1 == far - 1 and h == d):
                begin(ring_copy(s + 1, d, h, s))
            begin(peer_copy(s, d, h))

    def compute(b):
        for chunk in chunks(b):
            peer_copy(*chunk).wait_recv()
        count = 2 * tok
        block = pl.ds(count * b, count)
        marks = x[block, width : width + EXTRA].astype(jnp.float32)
        lane = lax.broadcasted_iota(jnp.int32, marks.shape, 1) % (EXTRA // 2)
        weight = jnp.sum(jnp.where(lane == chip, marks, 0.0), axis=1, keepdims=True)
        tile = min(256, ff)

        @pl.loop(0, ff // tile)
        def _(j):
            cols = pl.ds(pl.multiple_of(j * tile, tile), tile)
            rows_in = x[block, 0:width]
            gated = jnp.dot(rows_in, wg[:, cols], preferred_element_type=jnp.float32)
            upped = jnp.dot(rows_in, wu[:, cols], preferred_element_type=jnp.float32)
            act[:, cols] = (gated / (1.0 + jnp.exp(-gated)) * upped).astype(jnp.bfloat16)

        wide = min(512, width)

        @pl.loop(0, width // wide)
        def _(j):
            cols = pl.ds(pl.multiple_of(j * wide, wide), wide)
            product = jnp.dot(act[...], wd[:, cols], preferred_element_type=jnp.float32)
            part[block, cols] = (product * weight).astype(jnp.bfloat16)

        for chunk in chunks(b):
            begin(part_copy(*chunk))

    for h in range(2):
        here = slice(half * h, half * (h + 1))
        x[here, 0:width] = normalise(hidden[here, :], gain[...])
        if h == 0:
            pl.semaphore_wait(barrier, 3)
        begin(ring_copy(0, h, h, -1))
    for h in range(2):
        begin(ring_copy(0, 1 - h, h, -1))
        begin(peer_copy(-1, 0, h))
    forward(1)
    for load in loads:
        load.wait()
    for b in range(last - 1):
        compute(b)
        forward(b + 2)

    def place_of(s, d, h):
        return arrived.at[held(far - 1 if s < 0 and d else s, d, h)]

    def sum_copy(s, d, h):
        return pltpu.make_async_remote_copy(
            src_ref=part.at[rows(s, d, h)], dst_ref=place_of(s - 1, d, h),
            send_sem=rs_send.at[d, s, h], recv_sem=rs_recv.at[d, s, h],
            device_id={"expert": homeward[d]}, device_id_type=MESH)

    def local_sum(s, d, h):
        part_copy(s, d, h).wait_recv()
        mine = part[rows(s, d, h), :].astype(jnp.float32)
        return mine + peer_part[held(s, d, h), :].astype(jnp.float32)

    def send_sum(s, d, h):
        total = local_sum(s, d, h)
        if s < far - 2 or (s == far - 2 and h == d):
            sum_copy(s + 1, d, h).wait_recv()
            total += place_of(s, d, h)[...].astype(jnp.float32)
        part[rows(s, d, h), :] = total.astype(jnp.bfloat16)
        begin(sum_copy(s, d, h))

    compute(last - 1)
    for d in range(2):
        send_sum(far - 2, d, 1 - d)
    compute(last)
    for d in range(2):
        send_sum(far - 1, d, d)
    for d in range(2):
        send_sum(far - 2, d, d)
    for s in range(far - 3, -1, -1):
        for flip in (1, 0):
            for d in range(2):
                send_sum(s, d, d ^ flip)
    for h in (1, 0):
        total = local_sum(-1, 0, h)
        for d in range(2):
            sum_copy(0, d, h).wait_recv()
            total += place_of(-1, d, h)[...].astype(jnp.float32)
        here = slice(half * h, half * (h + 1))
        out[here, :] = (hidden[here, :].astype(jnp.float32) + total).astype(out.dtype)
    for copy in pending:
        copy.wait_send()


def vmem_need(tok, width, ff, chips):
    gathered = 2 * chips * tok
    return 2 * (gathered * (3 * width + EXTRA) + 3 * width * ff + 16 * tok * width)


def fused(snake, hidden, norm_gain, routes, gate_vals, span_len, w_gate, w_up, w_down):
    tok, width = hidden.shape
    ff = w_gate.shape[2]
    chips = lax.axis_size("expert") // 2
    far = chips // 2
    dma = pltpu.SemaphoreType.DMA
    in_vmem = pl.BlockSpec(memory_space=pltpu.VMEM)
    in_hbm = pl.BlockSpec(memory_space=pl.ANY)
    flops = 2 * 3 * 2 * chips * tok * width * ff
    return pl.pallas_call(
        functools.partial(kernel, chips, snake),
        out_shape=jax.ShapeDtypeStruct((tok, width), hidden.dtype),
        in_specs=[in_vmem] * 4 + [pl.BlockSpec(memory_space=pltpu.SMEM)] + [in_hbm] * 3,
        out_specs=in_vmem,
        scratch_shapes=[
            pltpu.VMEM((2 * chips * tok, width + EXTRA), jnp.bfloat16),
            pltpu.VMEM((2 * chips * tok, width), jnp.bfloat16),
            pltpu.VMEM((chips * tok, width), jnp.bfloat16),
            pltpu.VMEM((chips * tok, width), jnp.bfloat16),
            pltpu.VMEM((2 * tok, ff), jnp.bfloat16),
            pltpu.VMEM((width, ff), jnp.bfloat16),
            pltpu.VMEM((width, ff), jnp.bfloat16),
            pltpu.VMEM((ff, width), jnp.bfloat16),
            dma((3,)),
            dma((2, far, 2)), dma((2, far, 2)), dma((chips, 2)), dma((chips, 2)),
            dma((2, far, 2)), dma((2, far, 2)), dma((chips, 2)), dma((chips, 2)),
        ],
        compiler_params=pltpu.CompilerParams(
            collective_id=0, has_side_effects=True, vmem_limit_bytes=VMEM_BUDGET
        ),
        cost_estimate=pl.CostEstimate(
            flops=flops, bytes_accessed=6 * width * ff, transcendentals=2 * chips * tok * ff
        ),
    )(hidden, norm_gain, routes.T, gate_vals.T, span_len, w_gate, w_up, w_down)


def with_collectives(hidden, norm_gain, routes, gate_vals, span_len, w_gate, w_up, w_down):
    tok = hidden.shape[0]
    experts = lax.axis_size("expert") // 2
    me = lax.axis_index("expert")
    position = me * tok + jnp.arange(tok, dtype=jnp.int32)
    live = position % SEQ_TOK < span_len[position // SEQ_TOK]
    weights = gate_weights(routes.T, gate_vals.T, live[None, :], experts).T
    weights = lax.all_gather(weights, "expert", axis=0, tiled=True)
    mine = jnp.arange(experts, dtype=jnp.int32)[None, :] == me // 2
    weight = jnp.sum(jnp.where(mine, weights, 0.0), axis=1, keepdims=True)
    rows = lax.all_gather(normalise(hidden, norm_gain), "expert", axis=0, tiled=True)
    gated = jnp.dot(rows, w_gate[0], preferred_element_type=jnp.float32)
    upper = jnp.dot(rows, w_up[0], preferred_element_type=jnp.float32)
    act = (jax.nn.silu(gated) * upper).astype(jnp.bfloat16)
    part = jnp.dot(act, w_down[0], preferred_element_type=jnp.float32)
    part = (part * weight).astype(jnp.bfloat16)
    moe = lax.psum_scatter(part, "expert", scatter_dimension=0, tiled=True)
    return (hidden.astype(jnp.float32) + moe.astype(jnp.float32)).astype(jnp.bfloat16)


def solution(mesh):
    devices = mesh.shape["expert"]

    def on_device(hidden, *rest):
        tok, width = hidden.shape
        fits = vmem_need(tok, width, rest[-1].shape[1], devices // 2) <= VMEM_BUDGET - 2**23
        if fits and devices % 4 == 0 and devices >= 12 and SEQ_TOK % tok == 0 and tok % 32 == 0:
            return fused(devices == 16, hidden, *rest)
        return with_collectives(hidden, *rest)

    return jax.shard_map(
        on_device,
        mesh=mesh,
        in_specs=(
            P(("groups", "expert"), None),
            P(),
            P(("groups", "expert"), None),
            P(("groups", "expert"), None),
            P("groups"),
            P("expert", None, None),
            P("expert", None, None),
            P("expert", None, None),
        ),
        out_specs=P(("groups", "expert"), None),
        check_vma=False,
    )
```

time: 109 us -> 99.6 us (0.914)
  Pallas kernels: 103 us -> 97.6 us
  local copies, waits for them, and re-layouts: 5.93 us -> 1.87 us
    pallas_call x1, Pallas kernels: 103 us -> 97.6 us  [fused(): pl.pallas_call(functools.partial(kernel, chips, snake), out_shape=jax.Sha...]
    unnamed x3 -> x1, local copies, waits for them, and re-layouts: 4.62 us -> 1.87 us
    reshape x1 -> x0, local copies, waits for them, and re-layouts: 1.31 us -> none  [fused(): norm_gain.reshape(1, width)]
where the time goes in v3:
time: 99.6 us; the launch traced here: 99.5 us
  Pallas kernels  97.6 us (98%)
  local copies, waits for them, and re-layouts  1.87 us (2%)
    pallas_call x1, Pallas kernels, fused(): pl.pallas_call(functools.partial(kernel, chips, snake), out_shape=jax.Sha...  97.6 us

profile of v3, /device:TPU:0, one launch (start us, length us, event | category | flops | bytes accessed | tf_op | source)
XLA Modules:
  0.0 99.5 jit_solution(17510196551094216552)
XLA Ops:
  0.0 97.6 %shard_map.82 = bf16[64,4096]{1,0:T(8,128)(2,1)} custom-call(bf16[64,4096]{1,0:T(8,128)(2,1)} %hidden.1, bf16[4096]{0:T(1024)(128)(2,1)} %gain.1, s32[8,64]{1,0:T(8,128)} %bitcast.2, f32[8,64]{1,0:T(8,128)} %bitcast.3, s32[16]{0:T(128)} %span_len.1, bf16[1,4096,768]{2,1,0:T(8,128)(2,1)} %w_gate.1, bf16[1,4096,768]{2,1,0:T(8,128)(2,1)} %w_up.1, ...), custom_call_target="tpu_custom_call" | custom-call | flops 19327352832 | bytes 18874368 | tf_op jit(solution)/shard_map/pallas_call | solution.py:242
  97.6 1.9 %copy.10 = bf16[64,4096]{1,0:T(8,128)(2,1)} copy(bf16[64,4096]{1,0:T(8,128)(2,1)} %shard_map.82) | data formatting | bytes 1048576

commit v4 on v3

--- a/solution.py
+++ b/solution.py
@@ -153,7 +153,7 @@
             upped = jnp.dot(rows_in, wu[:, cols], preferred_element_type=jnp.float32)
             act[:, cols] = (gated / (1.0 + jnp.exp(-gated)) * upped).astype(jnp.bfloat16)
 
-        wide = min(512, width)
+        wide = min(1024, width)
 
         @pl.loop(0, width // wide)
         def _(j):
@@ -176,35 +176,43 @@
     forward(1)
     for load in loads:
         load.wait()
-    for b in range(last - 1):
+    compute(0)
+    for b in range(1, last):
         compute(b)
-        forward(b + 2)
-
-    def place_of(s, d, h):
-        return arrived.at[held(far - 1 if s < 0 and d else s, d, h)]
-
-    def sum_copy(s, d, h):
+        if b + 1 < last:
+            forward(b + 1)
+
+    def pieces(d, h):
+        return ((0, half // 2, h), (half // 2, half // 2, 2)) if h == d else ((0, half, h),)
+
+    def cut(block, piece):
+        return pl.ds(block.start + piece[0], piece[1])
+
+    def home(s, d, h):
+        return held(far - 1 if s < 0 and d else s, d, h)
+
+    def sum_copy(s, d, h, piece):
         return pltpu.make_async_remote_copy(
-            src_ref=part.at[rows(s, d, h)], dst_ref=place_of(s - 1, d, h),
-            send_sem=rs_send.at[d, s, h], recv_sem=rs_recv.at[d, s, h],
+            src_ref=part.at[cut(rows(s, d, h), piece)],
+            dst_ref=arrived.at[cut(home(s - 1, d, h), piece)],
+            send_sem=rs_send.at[d, s, piece[2]], recv_sem=rs_recv.at[d, s, piece[2]],
             device_id={"expert": homeward[d]}, device_id_type=MESH)
 
-    def local_sum(s, d, h):
+    def send_sum(s, d, h):
         part_copy(s, d, h).wait_recv()
-        mine = part[rows(s, d, h), :].astype(jnp.float32)
-        return mine + peer_part[held(s, d, h), :].astype(jnp.float32)
-
-    def send_sum(s, d, h):
-        total = local_sum(s, d, h)
-        if s < far - 2 or (s == far - 2 and h == d):
-            sum_copy(s + 1, d, h).wait_recv()
-            total += place_of(s, d, h)[...].astype(jnp.float32)
-        part[rows(s, d, h), :] = total.astype(jnp.bfloat16)
-        begin(sum_copy(s, d, h))
-
-    compute(last - 1)
+        for piece in pieces(d, h):
+            mine = cut(rows(s, d, h), piece)
+            total = part[mine, :].astype(jnp.float32)
+            total += peer_part[cut(held(s, d, h), piece), :].astype(jnp.float32)
+            if s < far - 2 or (s == far - 2 and h == d):
+                sum_copy(s + 1, d, h, piece).wait_recv()
+                total += arrived[cut(home(s, d, h), piece), :].astype(jnp.float32)
+            part[mine, :] = total.astype(jnp.bfloat16)
+            begin(sum_copy(s, d, h, piece))
+
     for d in range(2):
         send_sum(far - 2, d, 1 - d)
+    forward(last)
     compute(last)
     for d in range(2):
         send_sum(far - 1, d, d)
@@ -215,10 +223,13 @@
             for d in range(2):
                 send_sum(s, d, d ^ flip)
     for h in (1, 0):
-        total = local_sum(-1, 0, h)
+        part_copy(-1, 0, h).wait_recv()
+        total = part[rows(-1, 0, h), :].astype(jnp.float32)
+        total += peer_part[held(-1, 0, h), :].astype(jnp.float32)
         for d in range(2):
-            sum_copy(0, d, h).wait_recv()
-            total += place_of(-1, d, h)[...].astype(jnp.float32)
+            for piece in pieces(d, h):
+                sum_copy(0, d, h, piece).wait_recv()
+            total += arrived[home(-1, d, h), :].astype(jnp.float32)
         here = slice(half * h, half * (h + 1))
         out[here, :] = (hidden[here, :].astype(jnp.float32) + total).astype(out.dtype)
     for copy in pending:
@@ -255,7 +266,7 @@
             pltpu.VMEM((ff, width), jnp.bfloat16),
             dma((3,)),
             dma((2, far, 2)), dma((2, far, 2)), dma((chips, 2)), dma((chips, 2)),
-            dma((2, far, 2)), dma((2, far, 2)), dma((chips, 2)), dma((chips, 2)),
+            dma((2, far, 3)), dma((2, far, 3)), dma((chips, 2)), dma((chips, 2)),
         ],
         compiler_params=pltpu.CompilerParams(
             collective_id=0, has_side_effects=True, vmem_limit_bytes=VMEM_BUDGET
@@ -292,7 +303,7 @@
     def on_device(hidden, *rest):
         tok, width = hidden.shape
         fits = vmem_need(tok, width, rest[-1].shape[1], devices // 2) <= VMEM_BUDGET - 2**23
-        if fits and devices % 4 == 0 and devices >= 12 and SEQ_TOK % tok == 0 and tok % 32 == 0:
+        if fits and devices % 4 == 0 and devices >= 12 and SEQ_TOK % tok == 0 and tok % 64 == 0:
             return fused(devices == 16, hidden, *rest)
         return with_collectives(hidden, *rest)
 

time: 99.6 us -> 101 us (1.014)
  Pallas kernels: 97.6 us -> 99.4 us
    pallas_call x1, Pallas kernels: 97.6 us -> 99.4 us  [fused(): pl.pallas_call(functools.partial(kernel, chips, snake), out_shape=jax.Sha...]
where the time goes in v4:
time: 101 us
  Pallas kernels  99.4 us (98%)
  local copies, waits for them, and re-layouts  1.87 us (2%)
    pallas_call x1, Pallas kernels, fused(): pl.pallas_call(functools.partial(kernel, chips, snake), out_shape=jax.Sha...  99.4 us

profile of v4, /device:TPU:0, one launch (start us, length us, event | category | flops | bytes accessed | tf_op | source)
XLA Modules:
  0.0 101.3 jit_solution(6677519794171687616)
XLA Ops:
  0.0 99.4 %shard_map.82 = bf16[64,4096]{1,0:T(8,128)(2,1)} custom-call(bf16[64,4096]{1,0:T(8,128)(2,1)} %hidden.1, bf16[4096]{0:T(1024)(128)(2,1)} %gain.1, s32[8,64]{1,0:T(8,128)} %bitcast.2, f32[8,64]{1,0:T(8,128)} %bitcast.3, s32[16]{0:T(128)} %span_len.1, bf16[1,4096,768]{2,1,0:T(8,128)(2,1)} %w_gate.1, bf16[1,4096,768]{2,1,0:T(8,128)(2,1)} %w_up.1, ...), custom_call_target="tpu_custom_call" | custom-call | flops 19327352832 | bytes 18874368 | tf_op jit(solution)/shard_map/pallas_call | solution.py:253
  99.4 1.9 %copy.10 = bf16[64,4096]{1,0:T(8,128)(2,1)} copy(bf16[64,4096]{1,0:T(8,128)(2,1)} %shard_map.82) | data formatting | bytes 1048576
